TPU v7x, 256 devices: a whole 4x4x8 slice. The times are simulated.
256 devices in a mesh: chan: 64 (over x, z, core), src: 4 (over y).
Axes of the slice: x: 4, y: 4, z: 8, core: 2. Of those that a mesh axis runs over, the one named last changes fastest.
Arguments:
- records: bfloat16 [8192, 4096], P('chan'), may hold values from -600 to 600
- virtual_sources: int32 [64], P('src'), may hold values from 0 to 8191
- pair_group: int32 [32768, 1], P(('chan', 'src')), may hold values from 0 to 63; in each aligned block of 128 rows (0 to 127, 128 to 255, ...) at most 4 rows name the same one
- pair_receiver: int32 [32768], P(('chan', 'src')), may hold values from 0 to 127
- pair_source: int32 [32768], P(('chan', 'src')), may hold values from 0 to 15
- observed: float32 [32768, 2048], P(('chan', 'src')), may hold values from -6 to 6
Outputs:
- adjoint_source: float32 [8192, 4096], P(('chan', 'src'))
- pair_misfit: float32 [32768], P(('chan', 'src'))
Inputs may be any that keep to these rules, and one draw needn't show every extreme that they name: `pair_group`: among the 128 pairs listed by one device at most 4 name the same channel group, and in every draw some device lists exactly 4 pairs for some group.
All inputs are finite; a program needn't handle non-finite values.
Results may differ from a plain program's by a relative error of at most 0.0021.
Values sent between devices are 32-bit elements; how exact they have to be, the bound alone decides.
A program may use at most 64 MiB of HBM per device.

v0:
```python
import math
import jax
import jax.numpy as jnp
from jax import lax
from jax.sharding import PartitionSpec as P

K0 = 64


def fourier_basis(offset, length, time_len, bin_count):
    sample_times = offset + jnp.arange(length, dtype=jnp.int32)[:, None]
    band_bins = K0 + jnp.arange(bin_count, dtype=jnp.int32)[None, :]
    phase_index = band_bins * sample_times % (2 * time_len)
    angles = phase_index.astype(jnp.float32) * (math.pi / time_len)
    return jnp.concatenate([jnp.cos(angles), -jnp.sin(angles)], axis=1)


def forward(signal_rows, bin_count):
    time_len = signal_rows.shape[1]
    block_len = min(512, time_len)

    def add_block(block_index, running):
        offset = block_index * block_len
        segment = lax.dynamic_slice_in_dim(signal_rows, offset, block_len, 1)
        fourier_table = fourier_basis(offset, block_len, time_len, bin_count).astype(jnp.bfloat16)
        return running + jnp.dot(segment, fourier_table, preferred_element_type=jnp.float32)

    return lax.fori_loop(
        0,
        time_len // block_len,
        add_block,
        jnp.zeros((signal_rows.shape[0], 2 * bin_count), jnp.float32),
    )


def inverse(spectral, time_len):
    bin_count = spectral.shape[1] // 2
    block_len = min(512, time_len)

    def fill_block(block_index, output):
        offset = block_index * block_len
        fourier_table = fourier_basis(offset, block_len, time_len, bin_count)
        values = lax.dot_general(
            spectral,
            fourier_table,
            (((1,), (1,)), ((), ())),
            precision=lax.Precision.HIGHEST,
            preferred_element_type=jnp.float32,
        ) * (1.0 / math.sqrt(bin_count))
        return lax.dynamic_update_slice_in_dim(output, values, offset, 1)

    return lax.fori_loop(
        0, time_len // block_len, fill_block, jnp.zeros((spectral.shape[0], time_len), jnp.float32)
    )


def whiten(spectra):
    bin_count = spectra.shape[1] // 2
    band_power = jnp.sum(spectra * spectra, axis=1, keepdims=True) / bin_count
    return spectra / jnp.sqrt(band_power + 1e-06)


def band_taper(bin_count):
    band_bins = jnp.arange(bin_count, dtype=jnp.int32).astype(jnp.float32)
    return 0.5 - 0.5 * jnp.cos((band_bins + 0.5) * (2.0 * math.pi / bin_count))


def pair_terms(source_rows, receiver_rows, observed_rows):
    bin_count = observed_rows.shape[-1] // 2
    weights = band_taper(bin_count)
    source_real = source_rows[..., :bin_count]
    source_imag = source_rows[..., bin_count:]
    receiver_real = receiver_rows[..., :bin_count]
    receiver_imag = receiver_rows[..., bin_count:]
    corr_real = source_real * receiver_real + source_imag * receiver_imag
    corr_imag = source_real * receiver_imag - source_imag * receiver_real
    diff_real = corr_real - observed_rows[..., :bin_count]
    diff_imag = corr_imag - observed_rows[..., bin_count:]
    misfit = jnp.sum(weights * (diff_real * diff_real + diff_imag * diff_imag), axis=-1) / (
        2 * bin_count
    )
    resid_real = weights * diff_real
    resid_imag = weights * diff_imag
    term_real = resid_real * source_real - resid_imag * source_imag
    term_imag = resid_real * source_imag + resid_imag * source_real
    return (misfit, jnp.concatenate([term_real, term_imag], axis=-1))


def per_device(records, virtual_sources, pair_group, pair_receiver, pair_source, observed):
    row_count, time_len = records.shape
    pair_count = observed.shape[0]
    bin_count = observed.shape[1] // 2
    groups = lax.axis_size("chan")
    capacity = 2 * pair_count // groups
    slot_total = groups * capacity
    chan_index = lax.axis_index("chan")
    local_rows = virtual_sources - chan_index * row_count
    inside = (local_rows >= 0) & (local_rows < row_count)
    safe_rows = jnp.clip(local_rows, 0, row_count - 1)
    whitened = whiten(forward(records, bin_count))
    picked = jnp.where(inside[:, None], jnp.take(whitened, safe_rows, axis=0), 0.0)
    sources = lax.psum(picked, "chan")
    destination = pair_group[:, 0]
    group_hits = (destination[:, None] == jnp.arange(groups, dtype=jnp.int32)[None, :]).astype(
        jnp.int32
    )
    slot_ranks = jnp.sum((jnp.cumsum(group_hits, axis=0) - 1) * group_hits, axis=1)
    slot_index = destination * capacity + slot_ranks
    send_receiver = (
        jnp.full((slot_total,), -1, jnp.int32)
        .at[slot_index]
        .set(pair_receiver)
        .reshape(groups, capacity)
    )
    request = lax.all_to_all(send_receiver, "chan", split_axis=0, concat_axis=0, tiled=True)
    found_rows = jnp.take(whitened, jnp.clip(request, 0, row_count - 1), axis=0)
    found_rows = jnp.where((request >= 0)[..., None], found_rows, 0.0)
    fetched = lax.all_to_all(found_rows, "chan", split_axis=0, concat_axis=0, tiled=True)
    receiver_rows = fetched.reshape(slot_total, 2 * bin_count)[slot_index]
    source_rows = jnp.take(sources, pair_source, axis=0)
    pair_misfit, adjoint_term = pair_terms(source_rows, receiver_rows, observed)
    send_terms = (
        jnp.zeros((slot_total, 2 * bin_count), jnp.float32)
        .at[slot_index]
        .set(adjoint_term)
        .reshape(groups, capacity, 2 * bin_count)
    )
    arrived_terms, receivers = (
        lax.all_to_all(send_terms, "chan", split_axis=0, concat_axis=0, tiled=True),
        lax.all_to_all(send_receiver, "chan", split_axis=0, concat_axis=0, tiled=True),
    )
    flat_terms = arrived_terms.reshape(slot_total, 2 * bin_count)
    flat_receivers = receivers.reshape(slot_total)
    selector = (jnp.arange(row_count, dtype=jnp.int32)[:, None] == flat_receivers[None, :]).astype(
        jnp.float32
    )
    adjoint_spectra = jnp.dot(
        selector, flat_terms, precision=lax.Precision.HIGHEST, preferred_element_type=jnp.float32
    )
    adjoint_source = lax.psum_scatter(
        inverse(adjoint_spectra, time_len), "src", scatter_dimension=0, tiled=True
    )
    return (adjoint_source, pair_misfit)


def solution(mesh):
    return jax.shard_map(
        per_device,
        mesh=mesh,
        in_specs=(
            P("chan", None),
            P("src"),
            P(("chan", "src"), None),
            P(("chan", "src")),
            P(("chan", "src")),
            P(("chan", "src"), None),
        ),
        out_specs=(P(("chan", "src"), None), P(("chan", "src"))),
        check_vma=False,
    )
```

profile of v0, /device:TPU:1, one launch (start us, length us, event | category | flops | bytes accessed | tf_op | source)
XLA Modules:
  0.0 526.5 jit_solution(5404071709264893560)
XLA Ops:
  11.4 13.0 %all-to-all-start = ((s32[64,1,4]{2,1,0:T(1,128)}), s32[64,1,4]{2,1,0:T(1,128)S(1)}, u32[]{:S(2)}, u32[]{:S(2)}) async-start(s32[64,1,4]{2,1,0:T(1,128)} %bitcast.4), calls=%async_computation | async-start | bytes 65536 | tf_op jit(solution)/shard_map/all_to_all | solution.py:130
  24.4 85.0 %while.32 = (s32[]{:T(128)}, f32[128,2048]{1,0:T(8,128)S(1)}, bf16[128,4096]{1,0:T(8,128)(2,1)}, s32[]{:T(128)}, s32[]{:T(128)}, /*index=5*/s32[]{:T(128)}, s32[]{:T(128)}) while((s32[]{:T(128)}, f32[128,2048]{1,0:T(8,128)S(1)}, bf16[128,4096]{1,0:T(8,128)(2,1)}, s32[]{:T(128)}, s32[]{:T(128)}, /*index=5*/s32[]{:T(128)}, ...), condition=%wide.region_4.5_spmd.clone, body=%wide.region_3.4_spmd.clone.sunk | while | flops 282068480 | bytes 6434965 | solution.py:28
  24.5 9.0 %cosine_convert_fusion.2 = (bf16[512,1024]{1,0:T(8,128)(2,1)S(1)}, bf16[512,1024]{1,0:T(8,128)(2,1)S(1)}) fusion(s32[512]{0:T(512)S(1)} %iota_add_fusion.10, s32[1024]{0:T(1024)S(1)} %iota_add_fusion.11), kind=kLoop, calls=%fused_computation.39.clone.1 | loop fusion | flops 8912896 | bytes 2103296 | tf_op jit(solution)/shard_map/convert
  35.1 9.0 %cosine_convert_fusion.2 = (bf16[512,1024]{1,0:T(8,128)(2,1)S(1)}, bf16[512,1024]{1,0:T(8,128)(2,1)S(1)}) fusion(s32[512]{0:T(512)S(1)} %iota_add_fusion.10, s32[1024]{0:T(1024)S(1)} %iota_add_fusion.11), kind=kLoop, calls=%fused_computation.39.clone.1 | loop fusion | flops 8912896 | bytes 2103296 | tf_op jit(solution)/shard_map/convert
  45.7 9.0 %cosine_convert_fusion.2 = (bf16[512,1024]{1,0:T(8,128)(2,1)S(1)}, bf16[512,1024]{1,0:T(8,128)(2,1)S(1)}) fusion(s32[512]{0:T(512)S(1)} %iota_add_fusion.10, s32[1024]{0:T(1024)S(1)} %iota_add_fusion.11), kind=kLoop, calls=%fused_computation.39.clone.1 | loop fusion | flops 8912896 | bytes 2103296 | tf_op jit(solution)/shard_map/convert
  54.7 1.5 convolution_add_fusion.2
  56.3 9.0 %cosine_convert_fusion.2 = (bf16[512,1024]{1,0:T(8,128)(2,1)S(1)}, bf16[512,1024]{1,0:T(8,128)(2,1)S(1)}) fusion(s32[512]{0:T(512)S(1)} %iota_add_fusion.10, s32[1024]{0:T(1024)S(1)} %iota_add_fusion.11), kind=kLoop, calls=%fused_computation.39.clone.1 | loop fusion | flops 8912896 | bytes 2103296 | tf_op jit(solution)/shard_map/convert
  65.4 1.5 convolution_add_fusion.2
  67.0 9.0 %cosine_convert_fusion.2 = (bf16[512,1024]{1,0:T(8,128)(2,1)S(1)}, bf16[512,1024]{1,0:T(8,128)(2,1)S(1)}) fusion(s32[512]{0:T(512)S(1)} %iota_add_fusion.10, s32[1024]{0:T(1024)S(1)} %iota_add_fusion.11), kind=kLoop, calls=%fused_computation.39.clone.1 | loop fusion | flops 8912896 | bytes 2103296 | tf_op jit(solution)/shard_map/convert
  77.6 9.0 %cosine_convert_fusion.2 = (bf16[512,1024]{1,0:T(8,128)(2,1)S(1)}, bf16[512,1024]{1,0:T(8,128)(2,1)S(1)}) fusion(s32[512]{0:T(512)S(1)} %iota_add_fusion.10, s32[1024]{0:T(1024)S(1)} %iota_add_fusion.11), kind=kLoop, calls=%fused_computation.39.clone.1 | loop fusion | flops 8912896 | bytes 2103296 | tf_op jit(solution)/shard_map/convert
  86.6 1.5 convolution_add_fusion.2
  88.2 9.0 %cosine_convert_fusion.2 = (bf16[512,1024]{1,0:T(8,128)(2,1)S(1)}, bf16[512,1024]{1,0:T(8,128)(2,1)S(1)}) fusion(s32[512]{0:T(512)S(1)} %iota_add_fusion.10, s32[1024]{0:T(1024)S(1)} %iota_add_fusion.11), kind=kLoop, calls=%fused_computation.39.clone.1 | loop fusion | flops 8912896 | bytes 2103296 | tf_op jit(solution)/shard_map/convert
  97.3 1.5 convolution_add_fusion.2
  98.8 9.0 %cosine_convert_fusion.2 = (bf16[512,1024]{1,0:T(8,128)(2,1)S(1)}, bf16[512,1024]{1,0:T(8,128)(2,1)S(1)}) fusion(s32[512]{0:T(512)S(1)} %iota_add_fusion.10, s32[1024]{0:T(1024)S(1)} %iota_add_fusion.11), kind=kLoop, calls=%fused_computation.39.clone.1 | loop fusion | flops 8912896 | bytes 2103296 | tf_op jit(solution)/shard_map/convert
  107.9 1.5 convolution_add_fusion.2
  113.0 1.6 reshape.126
  114.6 3.6 select_select_fusion
  118.1 10.6 %all-to-all-start.1 = ((f32[64,4,2048]{2,1,0:T(4,128)}), f32[64,4,2048]{2,1,0:T(4,128)}, u32[]{:S(2)}, u32[]{:S(2)}) async-start(f32[64,4,2048]{2,1,0:T(4,128)} %select_select_fusion), calls=%async_computation.1 | async-start | bytes 4194304 | tf_op jit(solution)/shard_map/all_to_all | solution.py:118
  130.4 183.6 %all-reduce.2.cloned.1.call-done = f32[16,2048]{1,0:T(8,128)} async-done(((f32[16,2048]{1,0:T(8,128)}), f32[16,2048]{1,0:T(8,128)}) %all-reduce.2.cloned.1.call-update) | async-done | bytes 131088 | tf_op jit(solution)/shard_map/psum | solution.py:102
  314.0 2.4 gather_fusion.1
  316.5 2.0 reshape.106
  318.5 1.9 gather_fusion.3
  320.4 1.8 multiply_reduce_fusion.1
  322.5 1.8 scatter_custom_fusion.1
  324.3 1.7 reshape.107
  326.0 6.6 %all-to-all-start.2 = ((f32[64,4,2048]{2,1,0:T(4,128)}), f32[64,4,2048]{2,1,0:T(4,128)S(1)}, u32[]{:S(2)}, u32[]{:S(2)}) async-start(f32[64,4,2048]{2,1,0:T(4,128)} %reshape.107), calls=%async_computation.2 | async-start | bytes 4194304 | tf_op jit(solution)/shard_map/all_to_all | solution.py:129
  332.7 51.1 %all-to-all-done.2 = f32[64,4,2048]{2,1,0:T(4,128)S(1)} async-done(((f32[64,4,2048]{2,1,0:T(4,128)}), f32[64,4,2048]{2,1,0:T(4,128)S(1)}, u32[]{:S(2)}, u32[]{:S(2)}) %all-to-all-start.2) | async-done | bytes 2097184 | tf_op jit(solution)/shard_map/all_to_all | solution.py:129
  383.8 1.8 reshape.108
  385.6 2.5 fusion.29
  388.1 1.6 broadcast_in_dim.93.clone
  389.6 101.1 %while.31 = (s32[]{:T(128)}, f32[128,4096]{1,0:T(8,128)}, f32[128,2048]{1,0:T(8,128)S(1)}, s32[]{:T(128)}, s32[]{:T(128)}, /*index=5*/s32[]{:T(128)}, s32[]{:T(128)}) while((s32[]{:T(128)}, f32[128,4096]{1,0:T(8,128)}, f32[128,2048]{1,0:T(8,128)S(1)}, s32[]{:T(128)}, s32[]{:T(128)}, /*index=5*/s32[]{:T(128)}, s32[]{:T(128)}) %tuple.90), condition=%wide.region_9.10_spmd, body=%wide.region_8.9_spmd.sunk | while | flops 1619592704 | bytes 10760323 | solution.py:52
  389.7 8.3 %fusion.46 = (f32[512,1024]{1,0:T(8,128)S(1)}, f32[512,1024]{1,0:T(8,128)S(1)}) fusion(s32[512]{0:T(512)S(1)} %iota_add_fusion.8, s32[1024]{0:T(1024)S(1)} %iota_add_fusion.9), kind=kLoop, calls=%fused_computation.21.clone.1 | loop fusion | flops 7864320 | bytes 4200448 | tf_op jit(solution)/shard_map/while/body/eval_jaxpr/cos | solution.py:15
  398.0 3.4 fusion.47
  402.3 8.3 %fusion.46 = (f32[512,1024]{1,0:T(8,128)S(1)}, f32[512,1024]{1,0:T(8,128)S(1)}) fusion(s32[512]{0:T(512)S(1)} %iota_add_fusion.8, s32[1024]{0:T(1024)S(1)} %iota_add_fusion.9), kind=kLoop, calls=%fused_computation.21.clone.1 | loop fusion | flops 7864320 | bytes 4200448 | tf_op jit(solution)/shard_map/while/body/eval_jaxpr/cos | solution.py:15
  410.6 3.4 fusion.47
  415.0 8.3 %fusion.46 = (f32[512,1024]{1,0:T(8,128)S(1)}, f32[512,1024]{1,0:T(8,128)S(1)}) fusion(s32[512]{0:T(512)S(1)} %iota_add_fusion.8, s32[1024]{0:T(1024)S(1)} %iota_add_fusion.9), kind=kLoop, calls=%fused_computation.21.clone.1 | loop fusion | flops 7864320 | bytes 4200448 | tf_op jit(solution)/shard_map/while/body/eval_jaxpr/cos | solution.py:15
  423.3 3.4 fusion.47
  427.6 8.3 %fusion.46 = (f32[512,1024]{1,0:T(8,128)S(1)}, f32[512,1024]{1,0:T(8,128)S(1)}) fusion(s32[512]{0:T(512)S(1)} %iota_add_fusion.8, s32[1024]{0:T(1024)S(1)} %iota_add_fusion.9), kind=kLoop, calls=%fused_computation.21.clone.1 | loop fusion | flops 7864320 | bytes 4200448 | tf_op jit(solution)/shard_map/while/body/eval_jaxpr/cos | solution.py:15
  435.9 3.4 fusion.47
  440.3 8.3 %fusion.46 = (f32[512,1024]{1,0:T(8,128)S(1)}, f32[512,1024]{1,0:T(8,128)S(1)}) fusion(s32[512]{0:T(512)S(1)} %iota_add_fusion.8, s32[1024]{0:T(1024)S(1)} %iota_add_fusion.9), kind=kLoop, calls=%fused_computation.21.clone.1 | loop fusion | flops 7864320 | bytes 4200448 | tf_op jit(solution)/shard_map/while/body/eval_jaxpr/cos | solution.py:15
  448.6 3.4 fusion.47
  452.9 8.3 %fusion.46 = (f32[512,1024]{1,0:T(8,128)S(1)}, f32[512,1024]{1,0:T(8,128)S(1)}) fusion(s32[512]{0:T(512)S(1)} %iota_add_fusion.8, s32[1024]{0:T(1024)S(1)} %iota_add_fusion.9), kind=kLoop, calls=%fused_computation.21.clone.1 | loop fusion | flops 7864320 | bytes 4200448 | tf_op jit(solution)/shard_map/while/body/eval_jaxpr/cos | solution.py:15
  461.2 3.4 fusion.47
  465.5 8.3 %fusion.46 = (f32[512,1024]{1,0:T(8,128)S(1)}, f32[512,1024]{1,0:T(8,128)S(1)}) fusion(s32[512]{0:T(512)S(1)} %iota_add_fusion.8, s32[1024]{0:T(1024)S(1)} %iota_add_fusion.9), kind=kLoop, calls=%fused_computation.21.clone.1 | loop fusion | flops 7864320 | bytes 4200448 | tf_op jit(solution)/shard_map/while/body/eval_jaxpr/cos | solution.py:15
  473.8 3.4 fusion.47
  478.1 8.3 %fusion.46 = (f32[512,1024]{1,0:T(8,128)S(1)}, f32[512,1024]{1,0:T(8,128)S(1)}) fusion(s32[512]{0:T(512)S(1)} %iota_add_fusion.8, s32[1024]{0:T(1024)S(1)} %iota_add_fusion.9), kind=kLoop, calls=%fused_computation.21.clone.1 | loop fusion | flops 7864320 | bytes 4200448 | tf_op jit(solution)/shard_map/while/body/eval_jaxpr/cos | solution.py:15
  486.5 3.4 fusion.47
  491.3 28.4 %reduce-scatter.2.cloned.1.call-done = f32[32,4096]{1,0:T(8,128)} async-done(((f32[128,4096]{1,0:T(8,128)}), f32[32,4096]{1,0:T(8,128)}) %reduce-scatter.2.cloned.1.call-update) | async-done | bytes 524304 | tf_op jit(solution)/shard_map/reduce_scatter | solution.py:140
  (94 shorter events, 22.0 us)
Async XLA Ops:
  11.4 98.4 %all-to-all-start = ((s32[64,1,4]{2,1,0:T(1,128)}), s32[64,1,4]{2,1,0:T(1,128)S(1)}, u32[]{:S(2)}, u32[]{:S(2)}) async-start(s32[64,1,4]{2,1,0:T(1,128)} %bitcast.4), calls=%async_computation | async-start | bytes 65536 | tf_op jit(solution)/shard_map/all_to_all | solution.py:130
  118.1 10.7 %copy-start = (s32[16]{0:T(128)S(1)}, s32[16]{0:T(128)}, u32[]{:S(2)}) copy-start(s32[16]{0:T(128)} %param.11) | copy-start | bytes 196
  118.1 12.2 %copy-start.1 = (s32[128]{0:T(128)S(1)}, s32[128]{0:T(128)}, u32[]{:S(2)}) copy-start(s32[128]{0:T(128)} %param.14) | copy-start | bytes 1540
  118.1 198.3 %all-to-all-start.1 = ((f32[64,4,2048]{2,1,0:T(4,128)}), f32[64,4,2048]{2,1,0:T(4,128)}, u32[]{:S(2)}, u32[]{:S(2)}) async-start(f32[64,4,2048]{2,1,0:T(4,128)} %select_select_fusion), calls=%async_computation.1 | async-start | bytes 4194304 | tf_op jit(solution)/shard_map/all_to_all | solution.py:118
  128.8 185.2 %all-reduce.2.cloned.1.call-start = ((), (), s32[]{:S(2)}) async-start(), calls=%async_computation.4 | async-start | bytes 262144 | tf_op jit(solution)/shard_map/psum | solution.py:102
  326.0 57.9 %all-to-all-start.2 = ((f32[64,4,2048]{2,1,0:T(4,128)}), f32[64,4,2048]{2,1,0:T(4,128)S(1)}, u32[]{:S(2)}, u32[]{:S(2)}) async-start(f32[64,4,2048]{2,1,0:T(4,128)} %reshape.107), calls=%async_computation.2 | async-start | bytes 4194304 | tf_op jit(solution)/shard_map/all_to_all | solution.py:129
  332.6 187.1 %reduce-scatter.2.cloned.1.call-start = ((), (), s32[]{:S(2)}) async-start(), calls=%async_computation.5 | async-start | bytes 2621440 | tf_op jit(solution)/shard_map/reduce_scatter | solution.py:140
Sparse Core Ops, SparseCore 0:
  133.7 180.2 all-reduce.1
  490.9 28.7 reduce-scatter.1
where the time goes:
time: 527 us
  waiting for transfers between devices  263 us (50%)
  other arithmetic  151 us (29%)
  matrix products  42.2 us (8%)
  starting transfers between devices  30.3 us (6%)
  local copies, waits for them, and re-layouts  24.8 us (5%)
  between operations  14.3 us (3%)
    psum x1, waiting for transfers between devices, per_device(): sources = lax.psum(picked, 'chan')  184 us
    another operation x8, other arithmetic  72.2 us
    cos x8, other arithmetic, fourier_basis(): return jnp.concatenate([jnp.cos(angles), -jnp.sin(angles)], axis=1)  66.4 us
    all_to_all x1, waiting for transfers between devices, per_device(): lax.all_to_all(send_terms, 'chan', split_axis=0, concat_axis=0, tiled=True)  51.1 us
    reduce_scatter x1, waiting for transfers between devices, per_device(): lax.psum_scatter(inverse(adjoint_spectra, time_len), 'src', scatter_dimen...  28.4 us
    dot_general x8, matrix products, fill_block(): lax.dot_general(spectral, fourier_table, (((1,), (1,)), ((), ())), precis...  27.4 us
    all_to_all x1, starting transfers between devices, per_device(): lax.all_to_all(send_receiver, 'chan', split_axis=0, concat_axis=0, tiled=...  13 us
    dot_general x8, matrix products, add_block(): jnp.dot(segment, fourier_table, preferred_element_type=jnp.float32)  12.3 us
  transfers between devices with their start and end apart: 5, of which 3 were waited for; matrix products, arithmetic and copies ran while one was open for 17% of the time, Pallas kernels for 0%

commit v1 on v0

--- a/solution.py
+++ b/solution.py
@@ -99,7 +99,8 @@
     safe_rows = jnp.clip(local_rows, 0, row_count - 1)
     whitened = whiten(forward(records, bin_count))
     picked = jnp.where(inside[:, None], jnp.take(whitened, safe_rows, axis=0), 0.0)
-    sources = lax.psum(picked, "chan")
+    blocks = lax.all_gather(picked, "chan", axis=0, tiled=False)
+    sources = blocks.sum(axis=0)
     destination = pair_group[:, 0]
     group_hits = (destination[:, None] == jnp.arange(groups, dtype=jnp.int32)[None, :]).astype(
         jnp.int32

time: 527 us -> 417 us (0.79)
  waiting for transfers between devices: 263 us -> 148 us
  blocking collectives: 0 us -> 22.1 us
  starting transfers between devices: 30.3 us -> 14 us
    psum x1 -> x0, waiting for transfers between devices: 184 us -> none  [per_device(): sources = lax.psum(picked, 'chan')]
    all_to_all x1, waiting for transfers between devices: 0.01 us -> 65 us  [per_device(): lax.all_to_all(found_rows, 'chan', split_axis=0, concat_axis=0, tiled=True)]
    all_to_all x0 -> x1, blocking collectives: none -> 22.1 us  [per_device(): lax.all_to_all(send_receiver, 'chan', split_axis=0, concat_axis=0, tiled=...]
    all_to_all x1 -> x0, starting transfers between devices: 13 us -> none  [per_device(): lax.all_to_all(send_receiver, 'chan', split_axis=0, concat_axis=0, tiled=...]
  transfers between devices with their start and end apart: 5 -> 4, of which waited for: 3 -> 4; matrix products, arithmetic and copies ran while one was open for 17% -> 3% of each run, Pallas kernels for 0% -> 0%
where the time goes in v1:
time: 417 us; the launch traced here: 416 us
  other arithmetic  152 us (36%)
  waiting for transfers between devices  148 us (35%)
  matrix products  41.9 us (10%)
  local copies, waits for them, and re-layouts  23.2 us (6%)
  blocking collectives  22.1 us (5%)
  between operations  14.3 us (3%)
  starting transfers between devices  14 us (3%)
    another operation x8, other arithmetic  72.2 us
    cos x8, other arithmetic, fourier_basis(): return jnp.concatenate([jnp.cos(angles), -jnp.sin(angles)], axis=1)  66.4 us
    all_to_all x1, waiting for transfers between devices, per_device(): lax.all_to_all(found_rows, 'chan', split_axis=0, concat_axis=0, tiled=True)  65 us
    all_to_all x1, waiting for transfers between devices, per_device(): lax.all_to_all(send_terms, 'chan', split_axis=0, concat_axis=0, tiled=True)  51.1 us
    reduce_scatter x1, waiting for transfers between devices, per_device(): lax.psum_scatter(inverse(adjoint_spectra, time_len), 'src', scatter_dimen...  28.6 us
    dot_general x8, matrix products, fill_block(): lax.dot_general(spectral, fourier_table, (((1,), (1,)), ((), ())), precis...  27.4 us
    all_to_all x1, blocking collectives, per_device(): lax.all_to_all(send_receiver, 'chan', split_axis=0, concat_axis=0, tiled=...  22.1 us
    dot_general x8, matrix products, add_block(): jnp.dot(segment, fourier_table, preferred_element_type=jnp.float32)  12 us
  transfers between devices with their start and end apart: 4, of which 4 were waited for; matrix products, arithmetic and copies ran while one was open for 3% of the time, Pallas kernels for 0%

profile of v1, /device:TPU:1, one launch (start us, length us, event | category | flops | bytes accessed | tf_op | source)
XLA Modules:
  0.0 415.8 jit_solution(9492120250500539356)
XLA Ops:
  7.2 84.7 %while.32 = (s32[]{:T(128)}, f32[128,2048]{1,0:T(8,128)S(1)}, bf16[128,4096]{1,0:T(8,128)(2,1)}, s32[]{:T(128)}, s32[]{:T(128)}, /*index=5*/s32[]{:T(128)}, s32[]{:T(128)}) while((s32[]{:T(128)}, f32[128,2048]{1,0:T(8,128)S(1)}, bf16[128,4096]{1,0:T(8,128)(2,1)}, s32[]{:T(128)}, s32[]{:T(128)}, /*index=5*/s32[]{:T(128)}, ...), condition=%wide.region_4.5_spmd.clone, body=%wide.region_3.4_spmd.clone.sunk | while | flops 282068480 | bytes 6434957 | solution.py:28
  7.3 9.0 %cosine_convert_fusion.2 = (bf16[512,1024]{1,0:T(8,128)(2,1)S(1)}, bf16[512,1024]{1,0:T(8,128)(2,1)S(1)}) fusion(s32[512]{0:T(512)S(1)} %iota_add_fusion.10, s32[1024]{0:T(1024)S(1)} %iota_add_fusion.11), kind=kLoop, calls=%fused_computation.39.clone.1 | loop fusion | flops 8912896 | bytes 2103296 | tf_op jit(solution)/shard_map/convert
  16.3 1.5 convolution_add_fusion.2
  17.9 9.0 %cosine_convert_fusion.2 = (bf16[512,1024]{1,0:T(8,128)(2,1)S(1)}, bf16[512,1024]{1,0:T(8,128)(2,1)S(1)}) fusion(s32[512]{0:T(512)S(1)} %iota_add_fusion.10, s32[1024]{0:T(1024)S(1)} %iota_add_fusion.11), kind=kLoop, calls=%fused_computation.39.clone.1 | loop fusion | flops 8912896 | bytes 2103296 | tf_op jit(solution)/shard_map/convert
  26.9 1.5 convolution_add_fusion.2
  28.4 9.0 %cosine_convert_fusion.2 = (bf16[512,1024]{1,0:T(8,128)(2,1)S(1)}, bf16[512,1024]{1,0:T(8,128)(2,1)S(1)}) fusion(s32[512]{0:T(512)S(1)} %iota_add_fusion.10, s32[1024]{0:T(1024)S(1)} %iota_add_fusion.11), kind=kLoop, calls=%fused_computation.39.clone.1 | loop fusion | flops 8912896 | bytes 2103296 | tf_op jit(solution)/shard_map/convert
  37.5 1.5 convolution_add_fusion.2
  39.0 9.0 %cosine_convert_fusion.2 = (bf16[512,1024]{1,0:T(8,128)(2,1)S(1)}, bf16[512,1024]{1,0:T(8,128)(2,1)S(1)}) fusion(s32[512]{0:T(512)S(1)} %iota_add_fusion.10, s32[1024]{0:T(1024)S(1)} %iota_add_fusion.11), kind=kLoop, calls=%fused_computation.39.clone.1 | loop fusion | flops 8912896 | bytes 2103296 | tf_op jit(solution)/shard_map/convert
  49.6 9.0 %cosine_convert_fusion.2 = (bf16[512,1024]{1,0:T(8,128)(2,1)S(1)}, bf16[512,1024]{1,0:T(8,128)(2,1)S(1)}) fusion(s32[512]{0:T(512)S(1)} %iota_add_fusion.10, s32[1024]{0:T(1024)S(1)} %iota_add_fusion.11), kind=kLoop, calls=%fused_computation.39.clone.1 | loop fusion | flops 8912896 | bytes 2103296 | tf_op jit(solution)/shard_map/convert
  58.7 1.5 convolution_add_fusion.2
  60.2 9.0 %cosine_convert_fusion.2 = (bf16[512,1024]{1,0:T(8,128)(2,1)S(1)}, bf16[512,1024]{1,0:T(8,128)(2,1)S(1)}) fusion(s32[512]{0:T(512)S(1)} %iota_add_fusion.10, s32[1024]{0:T(1024)S(1)} %iota_add_fusion.11), kind=kLoop, calls=%fused_computation.39.clone.1 | loop fusion | flops 8912896 | bytes 2103296 | tf_op jit(solution)/shard_map/convert
  69.2 1.5 convolution_add_fusion.2
  70.8 9.0 %cosine_convert_fusion.2 = (bf16[512,1024]{1,0:T(8,128)(2,1)S(1)}, bf16[512,1024]{1,0:T(8,128)(2,1)S(1)}) fusion(s32[512]{0:T(512)S(1)} %iota_add_fusion.10, s32[1024]{0:T(1024)S(1)} %iota_add_fusion.11), kind=kLoop, calls=%fused_computation.39.clone.1 | loop fusion | flops 8912896 | bytes 2103296 | tf_op jit(solution)/shard_map/convert
  81.4 9.0 %cosine_convert_fusion.2 = (bf16[512,1024]{1,0:T(8,128)(2,1)S(1)}, bf16[512,1024]{1,0:T(8,128)(2,1)S(1)}) fusion(s32[512]{0:T(512)S(1)} %iota_add_fusion.10, s32[1024]{0:T(1024)S(1)} %iota_add_fusion.11), kind=kLoop, calls=%fused_computation.39.clone.1 | loop fusion | flops 8912896 | bytes 2103296 | tf_op jit(solution)/shard_map/convert
  90.4 1.5 convolution_add_fusion.2
  95.7 22.1 %all_to_all.20 = s32[64,1,4]{2,1,0:T(1,128)S(1)} all-to-all(s32[64,1,4]{2,1,0:T(1,128)S(1)} %bitcast.27), channel_id=1, replica_groups=mesh['chan'=64,'src'=4] {'chan'}, dimensions={0} | all-to-all | bytes 2048 | tf_op jit(solution)/shard_map/all_to_all | solution.py:131
  120.6 1.6 reshape.170
  122.5 3.6 select_select_fusion
  126.1 5.7 %all-to-all-start.1 = ((f32[64,4,2048]{2,1,0:T(4,128)}), f32[64,4,2048]{2,1,0:T(4,128)}, u32[]{:S(2)}, u32[]{:S(2)}) async-start(f32[64,4,2048]{2,1,0:T(4,128)} %select_select_fusion), calls=%async_computation.1 | async-start | bytes 4194304 | tf_op jit(solution)/shard_map/all_to_all | solution.py:119
  131.9 65.0 %all-to-all-done.1 = f32[64,4,2048]{2,1,0:T(4,128)} async-done(((f32[64,4,2048]{2,1,0:T(4,128)}), f32[64,4,2048]{2,1,0:T(4,128)}, u32[]{:S(2)}, u32[]{:S(2)}) %all-to-all-start.1) | async-done | bytes 2097184 | tf_op jit(solution)/shard_map/all_to_all | solution.py:119
  196.9 2.0 reshape.150
  199.9 3.5 all-gather.2.cloned.1.call-done
  203.3 3.8 reduce_sum.41
  210.0 1.8 scatter_custom_fusion.1
  211.8 1.7 reshape.151
  213.5 8.2 %all-to-all-start.2 = ((f32[64,4,2048]{2,1,0:T(4,128)}), f32[64,4,2048]{2,1,0:T(4,128)S(1)}, u32[]{:S(2)}, u32[]{:S(2)}) async-start(f32[64,4,2048]{2,1,0:T(4,128)} %reshape.151), calls=%async_computation.2 | async-start | bytes 4194304 | tf_op jit(solution)/shard_map/all_to_all | solution.py:130
  221.9 51.1 %all-to-all-done.2 = f32[64,4,2048]{2,1,0:T(4,128)S(1)} async-done(((f32[64,4,2048]{2,1,0:T(4,128)}), f32[64,4,2048]{2,1,0:T(4,128)S(1)}, u32[]{:S(2)}, u32[]{:S(2)}) %all-to-all-start.2) | async-done | bytes 2097184 | tf_op jit(solution)/shard_map/all_to_all | solution.py:130
  273.0 1.8 reshape.152
  274.8 2.5 fusion.30
  277.2 1.6 broadcast_in_dim.93.clone
  278.8 101.1 %while.31 = (s32[]{:T(128)}, f32[128,4096]{1,0:T(8,128)}, f32[128,2048]{1,0:T(8,128)S(1)}, s32[]{:T(128)}, s32[]{:T(128)}, /*index=5*/s32[]{:T(128)}, s32[]{:T(128)}) while((s32[]{:T(128)}, f32[128,4096]{1,0:T(8,128)}, f32[128,2048]{1,0:T(8,128)S(1)}, s32[]{:T(128)}, s32[]{:T(128)}, /*index=5*/s32[]{:T(128)}, s32[]{:T(128)}) %tuple.90), condition=%wide.region_9.10_spmd, body=%wide.region_8.9_spmd.sunk | while | flops 1619592704 | bytes 10760323 | solution.py:52
  278.8 8.3 %fusion.47 = (f32[512,1024]{1,0:T(8,128)S(1)}, f32[512,1024]{1,0:T(8,128)S(1)}) fusion(s32[512]{0:T(512)S(1)} %iota_add_fusion.8, s32[1024]{0:T(1024)S(1)} %iota_add_fusion.9), kind=kLoop, calls=%fused_computation.21.clone.1 | loop fusion | flops 7864320 | bytes 4200448 | tf_op jit(solution)/shard_map/while/body/eval_jaxpr/cos | solution.py:15
  287.1 3.4 fusion.48
  291.5 8.3 %fusion.47 = (f32[512,1024]{1,0:T(8,128)S(1)}, f32[512,1024]{1,0:T(8,128)S(1)}) fusion(s32[512]{0:T(512)S(1)} %iota_add_fusion.8, s32[1024]{0:T(1024)S(1)} %iota_add_fusion.9), kind=kLoop, calls=%fused_computation.21.clone.1 | loop fusion | flops 7864320 | bytes 4200448 | tf_op jit(solution)/shard_map/while/body/eval_jaxpr/cos | solution.py:15
  299.8 3.4 fusion.48
  304.1 8.3 %fusion.47 = (f32[512,1024]{1,0:T(8,128)S(1)}, f32[512,1024]{1,0:T(8,128)S(1)}) fusion(s32[512]{0:T(512)S(1)} %iota_add_fusion.8, s32[1024]{0:T(1024)S(1)} %iota_add_fusion.9), kind=kLoop, calls=%fused_computation.21.clone.1 | loop fusion | flops 7864320 | bytes 4200448 | tf_op jit(solution)/shard_map/while/body/eval_jaxpr/cos | solution.py:15
  312.4 3.4 fusion.48
  316.7 8.3 %fusion.47 = (f32[512,1024]{1,0:T(8,128)S(1)}, f32[512,1024]{1,0:T(8,128)S(1)}) fusion(s32[512]{0:T(512)S(1)} %iota_add_fusion.8, s32[1024]{0:T(1024)S(1)} %iota_add_fusion.9), kind=kLoop, calls=%fused_computation.21.clone.1 | loop fusion | flops 7864320 | bytes 4200448 | tf_op jit(solution)/shard_map/while/body/eval_jaxpr/cos | solution.py:15
  325.0 3.4 fusion.48
  329.4 8.3 %fusion.47 = (f32[512,1024]{1,0:T(8,128)S(1)}, f32[512,1024]{1,0:T(8,128)S(1)}) fusion(s32[512]{0:T(512)S(1)} %iota_add_fusion.8, s32[1024]{0:T(1024)S(1)} %iota_add_fusion.9), kind=kLoop, calls=%fused_computation.21.clone.1 | loop fusion | flops 7864320 | bytes 4200448 | tf_op jit(solution)/shard_map/while/body/eval_jaxpr/cos | solution.py:15
  337.7 3.4 fusion.48
  342.0 8.3 %fusion.47 = (f32[512,1024]{1,0:T(8,128)S(1)}, f32[512,1024]{1,0:T(8,128)S(1)}) fusion(s32[512]{0:T(512)S(1)} %iota_add_fusion.8, s32[1024]{0:T(1024)S(1)} %iota_add_fusion.9), kind=kLoop, calls=%fused_computation.21.clone.1 | loop fusion | flops 7864320 | bytes 4200448 | tf_op jit(solution)/shard_map/while/body/eval_jaxpr/cos | solution.py:15
  350.3 3.4 fusion.48
  354.7 8.3 %fusion.47 = (f32[512,1024]{1,0:T(8,128)S(1)}, f32[512,1024]{1,0:T(8,128)S(1)}) fusion(s32[512]{0:T(512)S(1)} %iota_add_fusion.8, s32[1024]{0:T(1024)S(1)} %iota_add_fusion.9), kind=kLoop, calls=%fused_computation.21.clone.1 | loop fusion | flops 7864320 | bytes 4200448 | tf_op jit(solution)/shard_map/while/body/eval_jaxpr/cos | solution.py:15
  363.0 3.4 fusion.48
  367.3 8.3 %fusion.47 = (f32[512,1024]{1,0:T(8,128)S(1)}, f32[512,1024]{1,0:T(8,128)S(1)}) fusion(s32[512]{0:T(512)S(1)} %iota_add_fusion.8, s32[1024]{0:T(1024)S(1)} %iota_add_fusion.9), kind=kLoop, calls=%fused_computation.21.clone.1 | loop fusion | flops 7864320 | bytes 4200448 | tf_op jit(solution)/shard_map/while/body/eval_jaxpr/cos | solution.py:15
  375.6 3.4 fusion.48
  380.4 28.6 %reduce-scatter.2.cloned.1.call-done = f32[32,4096]{1,0:T(8,128)} async-done(((f32[128,4096]{1,0:T(8,128)}), f32[32,4096]{1,0:T(8,128)}) %reduce-scatter.2.cloned.1.call-update) | async-done | bytes 524304 | tf_op jit(solution)/shard_map/reduce_scatter | solution.py:141
  (98 shorter events, 21.5 us)
Async XLA Ops:
  7.2 196.2 %all-gather.2.cloned.1.call-start = ((), (), s32[]{:S(2)}) async-start(), calls=%async_computation.4 | async-start | bytes 8519680 | tf_op jit(solution)/shard_map/all_gather | solution.py:102
  91.9 0.7 copy-start.2
  92.1 1.9 copy-start.1
  126.1 5.8 %copy-start.3 = (s32[128]{0:T(128)S(1)}, s32[128]{0:T(128)}, u32[]{:S(2)}) copy-start(s32[128]{0:T(128)} %param.14) | copy-start | bytes 1540
  126.1 70.8 %all-to-all-start.1 = ((f32[64,4,2048]{2,1,0:T(4,128)}), f32[64,4,2048]{2,1,0:T(4,128)}, u32[]{:S(2)}, u32[]{:S(2)}) async-start(f32[64,4,2048]{2,1,0:T(4,128)} %select_select_fusion), calls=%async_computation.1 | async-start | bytes 4194304 | tf_op jit(solution)/shard_map/all_to_all | solution.py:119
  208.1 1.2 copy-start
  213.5 59.5 %all-to-all-start.2 = ((f32[64,4,2048]{2,1,0:T(4,128)}), f32[64,4,2048]{2,1,0:T(4,128)S(1)}, u32[]{:S(2)}, u32[]{:S(2)}) async-start(f32[64,4,2048]{2,1,0:T(4,128)} %reshape.151), calls=%async_computation.2 | async-start | bytes 4194304 | tf_op jit(solution)/shard_map/all_to_all | solution.py:130
  221.7 187.3 %reduce-scatter.2.cloned.1.call-start = ((), (), s32[]{:S(2)}) async-start(), calls=%async_computation.5 | async-start | bytes 2621440 | tf_op jit(solution)/shard_map/reduce_scatter | solution.py:141
Sparse Core Ops, SparseCore 0:
  94.1 109.2 all-gather.1
  380.0 28.9 reduce-scatter.1
